TPU v7x, 512 devices: a whole 4x8x8 slice. The times are simulated.
512 devices in a mesh: coil: 16 (over x, z_hi, core), pencil: 32 (over z_lo, y).
Axes of the slice: x: 4, y: 8, z: 8 (z_hi: 2, z_lo: 4; z = z_hi * 4 + z_lo), core: 2. Of those that a mesh axis runs over, the one named last changes fastest.
Arguments:
- kspace: float32 [2, 32, 128, 64, 256], P(None, 'coil', 'pencil'), may hold values from -1.5 to 1.5
- sensitivity: bfloat16 [2, 32, 256, 256, 128], P(None, 'coil', 'pencil'), may hold values from -6 to 6
- line_index: int32 [128, 64], replicated, may hold values from 0 to 255, as said below
Outputs:
- adjoint_image: float32 [2, 256, 256, 128], P(None, 'pencil', 'coil')
Inputs may be any that keep to these rules, and one draw needn't show every extreme that they name: `line_index`: in every row, entry j lies in [j * 4, (j + 1) * 4), so a row's lines are distinct and ascending.
All inputs are finite; a program needn't handle non-finite values.
Results may differ from a plain program's by a relative error of at most 0.0003.
Values sent between devices are 32-bit elements; how exact they have to be, the bound alone decides.
A program may use at most 64 MiB of HBM per device.

v0:
```python
import functools
import math

import jax
import jax.numpy as jnp
import ml_dtypes
import numpy as np
from jax import lax
from jax.experimental import pallas as pl
from jax.experimental.pallas import tpu as pltpu
from jax.sharding import PartitionSpec as P

BF16 = jnp.bfloat16
F32 = jnp.float32
MESH = pl.DeviceIdType.MESH
WIDE = 2
NT = (((1,), (1,)), ((), ()))


def two_parts(values):
    high = values.astype(ml_dtypes.bfloat16)
    low = (values - high.astype(np.float64)).astype(ml_dtypes.bfloat16)
    return high, low


def wave(first, second, length):
    angle = (np.outer(first, second) % length) * (2.0 * math.pi / length)
    return np.cos(angle), np.sin(angle)


def readout_table(width, pencils):
    slab = width // pencils
    chunks = slab // WIDE
    cos, sin = wave(np.arange(width), np.arange(width), width)
    rows = np.stack([np.concatenate([cos, -sin], 1), np.concatenate([sin, cos], 1)])
    rows = rows.reshape(2, pencils, chunks, WIDE, 2 * width).transpose(2, 0, 3, 1, 4)
    high, low = two_parts(rows.reshape(chunks, 2 * WIDE * pencils, 2 * width))
    return np.concatenate([high, low, high], 2)


def phase_table(width, lines):
    group = width // lines
    freq = (np.arange(lines)[None, :] * group + np.arange(group)[:, None]).reshape(-1)
    cos, sin = wave(np.arange(width), freq, width)
    rows = np.concatenate([np.concatenate([cos, -sin], 1), np.concatenate([sin, cos], 1)], 0)
    high, low = two_parts(rows)
    return np.concatenate([high, low, high], 1)


def partition_table(width, scale):
    freq = np.arange(width).reshape(width // 2, 2).transpose(1, 0).reshape(-1)
    cos, sin = wave(freq, np.arange(width), width)
    rows = np.concatenate([np.concatenate([cos, sin], 1), np.concatenate([-sin, cos], 1)], 0)
    high, low = two_parts(rows * scale)
    return np.concatenate([high, low, high], 0)


def kernel(
    sizes,
    kspace_hbm,
    sens_hbm,
    lines_ref,
    wx_hbm,
    wy_hbm,
    wz_hbm,
    out_ref,
    kspace,
    sens,
    wx,
    wy,
    wz,
    parts,
    place,
    outbox,
    inbox,
    grid,
    planes,
    mixed,
    share,
    land1,
    land2,
    land3,
    load_sem,
    a_send,
    a_recv,
    s1,
    r1,
    s2,
    r2,
    s3,
    r3,
):
    pencils, coils, chunks, nx, ny, nz, lines = sizes
    ring = coils // 4
    deep = ny // coils
    coil = lax.axis_index("coil")
    me = lax.axis_index("pencil")
    core = coil % 2
    hi = (coil // 2) % 2
    col = coil // 4
    other_core = coil + 1 - 2 * core
    other_hi = coil + 2 - 4 * hi

    loads = [
        pltpu.make_async_copy(src, dst, load_sem.at[i])
        for i, (src, dst) in enumerate(
            [(kspace_hbm, kspace), (wx_hbm, wx), (wy_hbm, wy), (wz_hbm, wz), (sens_hbm, sens)]
        )
    ]
    for load in loads:
        load.start()

    barrier = pltpu.get_barrier_semaphore()

    def greet(to_coil, to_pencil):
        pl.semaphore_signal(
            barrier, inc=1, device_id=(to_coil, to_pencil), device_id_type=MESH
        )

    def greet_pencil(d, carry):
        greet(coil, (me + d) % pencils)
        return carry

    lax.fori_loop(1, pencils, greet_pencil, 0)
    greet(other_core, me)
    greet(other_hi, me)
    for d in range(1, ring):
        greet((coil + 4 * d) % coils, me)

    here = lines_ref[...] - (ny // lines) * lax.broadcasted_iota(jnp.int32, (nz, lines), 1)
    place[...] = jnp.concatenate([here, here], 1)

    loads[0].wait()
    for c in range(2):
        for comp in range(2):
            value = kspace[comp, c]
            high = value.astype(BF16)
            low = (value - high.astype(F32)).astype(BF16)
            parts[c, :, pl.ds(comp * nx, nx)] = high
            parts[c, :, pl.ds((2 + comp) * nx, nx)] = high
            parts[c, :, pl.ds((4 + comp) * nx, nx)] = low
    loads[1].wait()

    def readout(j):
        for c in range(2):
            result = lax.dot_general(wx[j], parts[c], NT, preferred_element_type=F32)
            for q in range(2 * WIDE):
                for zp in range(2):
                    outbox[j, pl.ds(zp * 8 + c * 4 + q, pencils, stride=16), :] = result[
                        q * pencils : (q + 1) * pencils, zp * 128 : (zp + 1) * 128
                    ]

    def a_copy(j, to, size, start):
        return pltpu.make_async_remote_copy(
            src_ref=outbox.at[j, pl.ds(start, size), :],
            dst_ref=inbox.at[j, pl.ds(pl.multiple_of(me * 16, 16) if size == 16 else 0, size), :],
            send_sem=a_send.at[j],
            recv_sem=a_recv.at[j],
            device_id=(coil, to),
            device_id_type=MESH,
        )

    def send(j):
        def one(d, carry):
            to = (me + d) % pencils
            a_copy(j, to, 16, pl.multiple_of(to * 16, 16)).start()
            return carry

        lax.fori_loop(1, pencils, one, 0)
        mine = pl.ds(pl.multiple_of(me * 16, 16), 16)
        inbox[j, mine, :] = outbox[j, mine, :]

    half = lax.broadcasted_iota(jnp.int32, (nz // 2, 128), 1) // 64

    def compute(j):
        for x in range(WIDE):
            for zl in range(2):
                spot = place[pl.ds(zl, nz // 2, stride=2), :]
                keep01 = spot == half
                keep23 = spot == half + 2
                for c in range(2):
                    for comp in range(2):
                        value = inbox[j, pl.ds(c * 4 + comp * 2 + x, nz // 2, stride=8), :]
                        turned = pltpu.roll(value, 64, 1)
                        if zl == 0:
                            both = jnp.where(half == 0, value, turned)
                        else:
                            both = jnp.where(half == 0, turned, value)
                        for k, keep in enumerate((keep01, keep23)):
                            kept = jnp.where(keep, both, 0.0)
                            high = kept.astype(BF16)
                            low = (kept - high.astype(F32)).astype(BF16)
                            rows = pl.ds(c * nz + zl * (nz // 2), nz // 2)
                            at = comp * ny + k * 128
                            grid[x, rows, pl.ds(at, 128)] = high
                            grid[x, rows, pl.ds(2 * ny + at, 128)] = high
                            grid[x, rows, pl.ds(4 * ny + at, 128)] = low
            planes[x] = lax.dot_general(wy[...], grid[x], NT, preferred_element_type=F32)
            for c in range(2):
                for comp in range(2):
                    value = planes[x, pl.ds(comp * ny, ny), pl.ds(c * nz, nz)]
                    high = value.astype(BF16)
                    low = (value - high.astype(F32)).astype(BF16)
                    rows = pl.ds(c * ny, ny)
                    mixed[x, rows, pl.ds(comp * nz, nz)] = high
                    mixed[x, rows, pl.ds((2 + comp) * nz, nz)] = high
                    mixed[x, rows, pl.ds((4 + comp) * nz, nz)] = low
            image = jnp.dot(mixed[x], wz[...], preferred_element_type=F32)
            for slab in range(coils):
                real_part = 0.0
                imag_part = 0.0
                for c in range(2):
                    at = c * ny + slab * deep
                    re = image[at : at + deep, :nz]
                    im = image[at : at + deep, nz:]
                    rows = pl.ds(slab * deep, deep)
                    sre = sens[0, c, j * WIDE + x, rows, :].astype(F32)
                    sim = sens[1, c, j * WIDE + x, rows, :].astype(F32)
                    real_part = real_part + sre * re + sim * im
                    imag_part = imag_part + sre * im - sim * re
                where = (slab % 2, slab // 4, (slab // 2) % 2)
                share[(j,) + where + (0, x)] = real_part
                share[(j,) + where + (1, x)] = imag_part

    def copy1(j):
        return pltpu.make_async_remote_copy(
            src_ref=share.at[j, 1 - core],
            dst_ref=land1.at[j],
            send_sem=s1.at[j],
            recv_sem=r1.at[j],
            device_id=(other_core, me),
            device_id_type=MESH,
        )

    def copy2(j, d):
        return pltpu.make_async_remote_copy(
            src_ref=share.at[j, core, (col + d) % ring],
            dst_ref=land2.at[j, d - 1],
            send_sem=s2.at[j],
            recv_sem=r2.at[j],
            device_id=((coil + 4 * d) % coils, me),
            device_id_type=MESH,
        )

    def all2(j):
        return pltpu.make_async_remote_copy(
            src_ref=land2.at[j],
            dst_ref=land2.at[j],
            send_sem=s2.at[j],
            recv_sem=r2.at[j],
            device_id=((coil + 4) % coils, me),
            device_id_type=MESH,
        )

    def copy3(j):
        return pltpu.make_async_remote_copy(
            src_ref=share.at[j, core, col, 1 - hi],
            dst_ref=land3.at[j],
            send_sem=s3.at[j],
            recv_sem=r3.at[j],
            device_id=(other_hi, me),
            device_id_type=MESH,
        )

    def step2(j):
        copy1(j).wait_recv()
        share[j, core] = share[j, core] + land1[j]
        for d in range(1, ring):
            copy2(j, d).start()

    def step3(j):
        all2(j).wait_recv()
        total = share[j, core, col]
        for d in range(ring - 1):
            total = total + land2[j, d]
        share[j, core, col] = total
        copy3(j).start()

    def step4(j):
        copy3(j).wait_recv()
        total = share[j, core, col, hi] + land3[j]
        for x in range(WIDE):
            for comp in range(2):
                out_ref[comp, j * WIDE + x] = total[comp, x]

    readout(0)
    pl.semaphore_wait(barrier, pencils + ring)
    send(0)

    def early(j, carry):
        readout(j)
        send(j)
        return carry

    lax.fori_loop(1, chunks, early, 0)
    for load in loads[2:]:
        load.wait()

    def turn(j, carry):
        a_copy(j, me, (pencils - 1) * 16, 0).wait_recv()
        compute(j)
        copy1(j).start()

        @pl.when(j >= 1)
        def _():
            step3(j - 1)

        step2(j)

        @pl.when(j >= 2)
        def _():
            step4(j - 2)

        return carry

    lax.fori_loop(0, chunks, turn, 0)
    step4(chunks - 2)
    step3(chunks - 1)

    def drain(j, carry):
        a_copy(j, me, (pencils - 1) * 16, 0).wait_send()
        copy1(j).wait_send()
        all2(j).wait_send()
        copy3(j).wait_send()
        return carry

    lax.fori_loop(0, chunks, drain, 0)
    step4(chunks - 1)


def on_device(coils, pencils, kspace, sensitivity, line_index):
    _, coil_dev, part_dev, lines, nx = kspace.shape
    slab, ny, nz = sensitivity.shape[2:]
    chunks = slab // WIDE
    ring = coils // 4
    deep = ny // coils
    sizes = (pencils, coils, chunks, nx, ny, nz, lines)
    scale = 1.0 / math.sqrt(nx * ny * nz)
    rows = part_dev * lines
    wx = jnp.asarray(readout_table(nx, pencils))
    wy = jnp.asarray(phase_table(ny, lines))
    wz = jnp.asarray(partition_table(nz, scale))
    block = (2, WIDE, deep, nz)
    vmem = pltpu.VMEM
    dma = pltpu.SemaphoreType.DMA
    flat = kspace.reshape(2, coil_dev, rows, nx)
    return pl.pallas_call(
        functools.partial(kernel, sizes),
        out_shape=jax.ShapeDtypeStruct((2, slab, deep, nz), F32),
        in_specs=[
            pl.BlockSpec(memory_space=pl.ANY),
            pl.BlockSpec(memory_space=pl.ANY),
            pl.BlockSpec(memory_space=pltpu.VMEM),
            pl.BlockSpec(memory_space=pl.ANY),
            pl.BlockSpec(memory_space=pl.ANY),
            pl.BlockSpec(memory_space=pl.ANY),
        ],
        out_specs=pl.BlockSpec(memory_space=pltpu.VMEM),
        scratch_shapes=[
            vmem(flat.shape, F32),
            vmem(sensitivity.shape, BF16),
            vmem(wx.shape, BF16),
            vmem(wy.shape, BF16),
            vmem(wz.shape, BF16),
            vmem((coil_dev, rows, 6 * nx), BF16),
            vmem((nz, 2 * lines), jnp.int32),
            vmem((chunks, pencils * 16, 128), F32),
            vmem((chunks, pencils * 16, 128), F32),
            vmem((WIDE, coil_dev * nz, 6 * ny), BF16),
            vmem((WIDE, 2 * ny, coil_dev * nz), F32),
            vmem((WIDE, coil_dev * ny, 6 * nz), BF16),
            vmem((chunks, 2, ring, 2) + block, F32),
            vmem((chunks, ring, 2) + block, F32),
            vmem((chunks, ring - 1, 2) + block, F32),
            vmem((chunks,) + block, F32),
            dma((5,)),
        ]
        + [dma((chunks,)) for _ in range(8)],
        compiler_params=pltpu.CompilerParams(
            collective_id=0, has_side_effects=True, vmem_limit_bytes=48 * 1024 * 1024
        ),
    )(flat, sensitivity, line_index, wx, wy, wz)


def solution(mesh):
    in_specs = (P(None, "coil", "pencil", None, None), P(None, "coil", "pencil", None, None), P())
    out_specs = P(None, "pencil", "coil", None)
    return jax.shard_map(
        functools.partial(on_device, mesh.shape["coil"], mesh.shape["pencil"]),
        mesh=mesh,
        in_specs=in_specs,
        out_specs=out_specs,
        check_vma=False,
    )
```

profile of v0, /device:TPU:1, one launch (start us, length us, event | category | flops | bytes accessed | tf_op | source)
XLA Modules:
  0.0 72.0 jit_solution(12340227519625627668)
XLA Ops:
  0.0 0.8 %copy.7.lines_ref = s32[128,64]{1,0:T(8,128)S(1)} copy(s32[128,64]{0,1:T(8,128)} %param.8) | data formatting | bytes 65536 | tf_op args[2]
  0.9 0.0 copy-start
  0.9 1.4 %copy-done = bf16[512,1536]{1,0:T(8,128)(2,1)S(1)} copy-done((bf16[512,1536]{1,0:T(8,128)(2,1)S(1)}, bf16[512,1536]{1,0:T(8,128)(2,1)}, u32[]{:S(2)}) %copy-start) | copy-done | bytes 1572888
  2.3 0.0 copy-start.1
  2.3 1.4 %copy-done.1 = bf16[4,128,1536]{2,1,0:T(8,128)(2,1)S(1)} copy-done((bf16[4,128,1536]{2,1,0:T(8,128)(2,1)S(1)}, bf16[4,128,1536]{2,1,0:T(8,128)(2,1)}, u32[]{:S(2)}) %copy-start.1) | copy-done | bytes 1572888
  3.7 0.0 copy-start.2
  3.7 1.2 %copy-done.2 = f32[2,2,4,64,256]{4,3,2,1,0:T(8,128)S(1)} copy-done((f32[2,2,4,64,256]{4,3,2,1,0:T(8,128)S(1)}, f32[2,2,4,64,256]{4,3,2,1,0:T(8,128)}, u32[]{:S(2)}) %copy-start.2) | copy-done | bytes 1048600
  4.9 0.0 copy-start.3
  4.9 1.0 %copy-done.3 = bf16[768,256]{1,0:T(8,128)(2,1)S(1)} copy-done((bf16[768,256]{1,0:T(8,128)(2,1)S(1)}, bf16[768,256]{1,0:T(8,128)(2,1)}, u32[]{:S(2)}) %copy-start.3) | copy-done | bytes 393240
  5.9 65.4 %shard_map.64 = f32[2,8,16,128]{3,2,1,0:T(8,128)S(1)} custom-call(f32[2,2,256,256]{3,2,1,0:T(8,128)S(1)} %bitcast.1, bf16[2,2,8,256,128]{4,3,2,1,0:T(8,128)(2,1)} %sens_hbm.1, s32[128,64]{1,0:T(8,128)S(1)} %copy.7.lines_ref, bf16[4,128,1536]{2,1,0:T(8,128)(2,1)S(1)} %copy-done.1, bf16[512,1536]{1,0:T(8,128)(2,1)S(1)} %copy-done, bf16[768,256]{1,0:T(8,128)(2,1)S(1)} %copy-done.3), custom_call_target="tpu_custom_call" | custom-call | tf_op jit(solution)/shard_map/pallas_call | solution.py:347
  71.3 0.7 copy.9
Async XLA Ops:
  0.9 1.4 %copy-start = (bf16[512,1536]{1,0:T(8,128)(2,1)S(1)}, bf16[512,1536]{1,0:T(8,128)(2,1)}, u32[]{:S(2)}) copy-start(bf16[512,1536]{1,0:T(8,128)(2,1)} %constant.7.clone.wy_hbm) | copy-start | bytes 4718596
  2.3 1.4 %copy-start.1 = (bf16[4,128,1536]{2,1,0:T(8,128)(2,1)S(1)}, bf16[4,128,1536]{2,1,0:T(8,128)(2,1)}, u32[]{:S(2)}) copy-start(bf16[4,128,1536]{2,1,0:T(8,128)(2,1)} %constant.6.clone.wx_hbm) | copy-start | bytes 4718596
  3.7 1.2 %copy-start.2 = (f32[2,2,4,64,256]{4,3,2,1,0:T(8,128)S(1)}, f32[2,2,4,64,256]{4,3,2,1,0:T(8,128)}, u32[]{:S(2)}) copy-start(f32[2,2,4,64,256]{4,3,2,1,0:T(8,128)} %param.6) | copy-start | bytes 3145732
  4.9 1.0 %copy-start.3 = (bf16[768,256]{1,0:T(8,128)(2,1)S(1)}, bf16[768,256]{1,0:T(8,128)(2,1)}, u32[]{:S(2)}) copy-start(bf16[768,256]{1,0:T(8,128)(2,1)} %constant.8.clone.wz_hbm) | copy-start | bytes 1179652
where the time goes:
time: 72.3 us; the launch traced here: 72 us
  Pallas kernels  65.4 us (90%)
  local copies, waits for them, and re-layouts  6.54 us (9%)
    pallas_call x1, Pallas kernels, on_device(): pl.pallas_call(functools.partial(kernel, sizes), out_shape=jax.ShapeDtype...  65.4 us
    unnamed x10, local copies, waits for them, and re-layouts  6.54 us

commit v1 on v0

v1 whole, which is shorter than its diff:
```python
import functools
import math

import jax
import jax.numpy as jnp
import ml_dtypes
import numpy as np
from jax import lax
from jax.experimental import pallas as pl
from jax.experimental.pallas import tpu as pltpu
from jax.sharding import PartitionSpec as P

BF16 = jnp.bfloat16
F32 = jnp.float32
MESH = pl.DeviceIdType.MESH
WIDE = 2
RING_Y = 8
BLOCK = 8
NT = (((1,), (1,)), ((), ()))


def two_parts(values):
    high = values.astype(ml_dtypes.bfloat16)
    low = (values - high.astype(np.float64)).astype(ml_dtypes.bfloat16)
    return high, low


def wave(first, second, length):
    angle = (np.outer(first, second) % length) * (2.0 * math.pi / length)
    return np.cos(angle), np.sin(angle)


def readout_table(width, pencils):
    slab = width // pencils
    chunks = slab // WIDE
    cos, sin = wave(np.arange(width), np.arange(width), width)
    rows = np.stack([np.concatenate([cos, -sin], 1), np.concatenate([sin, cos], 1)])
    rows = rows.reshape(2, pencils, chunks, WIDE, 2 * width).transpose(2, 3, 0, 1, 4)
    high, low = two_parts(rows.reshape(chunks, 2 * WIDE * pencils, 2 * width))
    return np.concatenate([high, low, high], 2)


def phase_table(width, lines, slabs):
    group = width // lines
    freq = (np.arange(lines)[None, :] * group + np.arange(group)[:, None]).reshape(-1)
    cos, sin = wave(np.arange(width), freq, width)
    rows = np.stack([np.concatenate([cos, -sin], 1), np.concatenate([sin, cos], 1)])
    rows = rows.reshape(2, slabs // 2, 2, width // slabs, 2 * width).transpose(2, 0, 1, 3, 4)
    high, low = two_parts(rows.reshape(2, width, 2 * width))
    return np.concatenate([high, low, high], 2)


def partition_table(width, scale):
    freq = np.arange(width).reshape(width // 2, 2).transpose(1, 0).reshape(-1)
    cos, sin = wave(freq, np.arange(width), width)
    rows = np.concatenate([np.concatenate([cos, sin], 1), np.concatenate([-sin, cos], 1)], 0)
    high, low = two_parts(rows * scale)
    return np.concatenate([high, low, high], 0)


def kernel(
    sizes,
    kspace_hbm,
    sens_hbm,
    lines_ref,
    wx_hbm,
    wy_hbm,
    wz_hbm,
    out_ref,
    kspace,
    sens,
    wx,
    wy,
    wz,
    parts,
    place,
    outbox,
    inbox,
    grid,
    planes,
    mixed,
    share,
    land1,
    land2,
    land3,
    land4,
    load_sem,
    a_send,
    a_recv,
    s1,
    r1,
    s2,
    r2,
    s3,
    r3,
    s4,
):
    pencils, coils, chunks, nx, ny, nz, lines = sizes
    ring = coils // 4
    deep = ny // coils
    coil = lax.axis_index("coil")
    me = lax.axis_index("pencil")
    core = coil % 2
    hi = coil // 2 % 2
    col = coil // 4
    other_core = coil + 1 - 2 * core
    other_hi = coil + 2 - 4 * hi

    loads = [
        pltpu.make_async_copy(src, dst, load_sem.at[i])
        for i, (src, dst) in enumerate(
            [(kspace_hbm, kspace), (wx_hbm, wx), (wy_hbm, wy), (wz_hbm, wz), (sens_hbm, sens)]
        )
    ]
    for load in loads[:2]:
        load.start()

    barrier = pltpu.get_barrier_semaphore()

    def greet(to_coil, to_pencil):
        pl.semaphore_signal(
            barrier, inc=1, device_id=(to_coil, to_pencil), device_id_type=MESH
        )

    def greet_pencil(d, carry):
        greet(coil, (me + d) % pencils)
        return carry

    lax.fori_loop(1, pencils, greet_pencil, 0)
    greet(other_core, me)
    for d in range(1, coils // 2):
        greet((coil + 2 * d) % coils, me)

    here = lines_ref[...] - (ny // lines) * lax.broadcasted_iota(jnp.int32, (lines, nz), 0)
    place[...] = jnp.concatenate([here, here], 0).T

    loads[0].wait()
    for load in loads[2:]:
        load.start()
    for c in range(2):
        for comp in range(2):
            value = kspace[comp, c]
            high = value.astype(BF16)
            low = (value - high.astype(F32)).astype(BF16)
            parts[c, :, pl.ds(comp * nx, nx)] = high
            parts[c, :, pl.ds((2 + comp) * nx, nx)] = high
            parts[c, :, pl.ds((4 + comp) * nx, nx)] = low
    loads[1].wait()

    def readout(j):
        for c in range(2):
            result = lax.dot_general(wx[j], parts[c], NT, preferred_element_type=F32)
            for x in range(WIDE):
                for comp in range(2):
                    rows = (x * 2 + comp) * pencils
                    for zp in range(2):
                        to = pl.ds(zp * 4 + c * 2 + comp, pencils, stride=BLOCK)
                        outbox[j * WIDE + x, to, :] = result[
                            rows : rows + pencils, zp * 128 : (zp + 1) * 128
                        ]

    def at(pencil):
        return pl.ds(pl.multiple_of(pencil * BLOCK, BLOCK), BLOCK)

    def a_copy(x, count, to):
        return pltpu.make_async_remote_copy(
            src_ref=outbox.at[pl.ds(x, count), at(to), :],
            dst_ref=inbox.at[pl.ds(x, count), at(me), :],
            send_sem=a_send.at[x],
            recv_sem=a_recv.at[x],
            device_id=(coil, to),
            device_id_type=MESH,
        )

    def a_many(x, count):
        return pltpu.make_async_remote_copy(
            src_ref=outbox.at[pl.ds(x, count), pl.ds(0, (pencils - 1) * BLOCK), :],
            dst_ref=inbox.at[pl.ds(x, count), pl.ds(0, (pencils - 1) * BLOCK), :],
            send_sem=a_send.at[x],
            recv_sem=a_recv.at[x],
            device_id=(coil, me),
            device_id_type=MESH,
        )

    def send(x, count):
        def one(i, carry):
            k, g = i // RING_Y, i % RING_Y
            dy = 1 + g // 4 + 4 * (g % 2) + 2 * (g % 4 // 2)
            dz = k + g + 2
            to = (me // RING_Y + dz) % (pencils // RING_Y) * RING_Y + (me + dy) % RING_Y
            a_copy(x, count, to).start()
            return carry

        lax.fori_loop(0, pencils - 1, one, 0)
        for k in range(count):
            inbox[x + k, at(me), :] = outbox[x + k, at(me), :]

    half = lax.broadcasted_iota(jnp.int32, (nz // 2, 128), 1) // 64

    def fill(x, buf):
        for zl in range(2):
            spot = place[pl.ds(zl, nz // 2, stride=2), :]
            keep01 = spot == half
            keep23 = spot == half + 2
            for c in range(2):
                for comp in range(2):
                    value = inbox[x, pl.ds(c * 2 + comp, nz // 2, stride=4), :]
                    turned = pltpu.roll(value, 64, 1)
                    if zl == 0:
                        both = jnp.where(half == 0, value, turned)
                    else:
                        both = jnp.where(half == 0, turned, value)
                    for k, keep in enumerate((keep01, keep23)):
                        kept = jnp.where(keep, both, 0.0)
                        high = kept.astype(BF16)
                        low = (kept - high.astype(F32)).astype(BF16)
                        rows = pl.ds(c * nz + zl * (nz // 2), nz // 2)
                        left = comp * ny + k * 128
                        grid[buf, rows, pl.ds(left, 128)] = high
                        grid[buf, rows, pl.ds(2 * ny + left, 128)] = high
                        grid[buf, rows, pl.ds(4 * ny + left, 128)] = low

    def combine(x, buf):
        tall = ny // 2
        table = wy[...].reshape(2 * ny, 6 * ny)
        planes[...] = lax.dot_general(table, grid[buf], NT, preferred_element_type=F32)
        for part in range(2):
            for c in range(2):
                for comp in range(2):
                    value = planes[pl.ds(part * ny + comp * tall, tall), pl.ds(c * nz, nz)]
                    high = value.astype(BF16)
                    low = (value - high.astype(F32)).astype(BF16)
                    rows = pl.ds(part * ny + c * tall, tall)
                    mixed[rows, pl.ds(comp * nz, nz)] = high
                    mixed[rows, pl.ds((2 + comp) * nz, nz)] = high
                    mixed[rows, pl.ds((4 + comp) * nz, nz)] = low
        image = jnp.dot(mixed[...], wz[...], preferred_element_type=F32)
        for part in range(2):
            for m in range(coils // 2):
                real_part = 0.0
                imag_part = 0.0
                for c in range(2):
                    top = part * ny + c * tall + m * deep
                    re = image[top : top + deep, :nz]
                    im = image[top : top + deep, nz:]
                    rows = pl.ds((2 * m + part) * deep, deep)
                    sre = sens[0, c, x, rows, :].astype(F32)
                    sim = sens[1, c, x, rows, :].astype(F32)
                    real_part = real_part + sre * re + sim * im
                    imag_part = imag_part + sre * im - sim * re
                share[x, part, m // 2, m % 2, 0] = real_part
                share[x, part, m // 2, m % 2, 1] = imag_part

    def compute(x, buf):
        fill(x, buf)
        combine(x, buf)
        copy1(x).start()

    def copy1(j):
        return pltpu.make_async_remote_copy(
            src_ref=share.at[j, 1 - core],
            dst_ref=land1.at[j],
            send_sem=s1.at[j],
            recv_sem=r1.at[j],
            device_id=(other_core, me),
            device_id_type=MESH,
        )

    def copy2(j, d):
        return pltpu.make_async_remote_copy(
            src_ref=share.at[j, core, (col + d) % ring],
            dst_ref=land2.at[j, d - 1],
            send_sem=s2.at[j],
            recv_sem=r2.at[j],
            device_id=((coil + 4 * d) % coils, me),
            device_id_type=MESH,
        )

    def all2(j):
        return pltpu.make_async_remote_copy(
            src_ref=land2.at[j],
            dst_ref=land2.at[j],
            send_sem=s2.at[j],
            recv_sem=r2.at[j],
            device_id=((coil + 4) % coils, me),
            device_id_type=MESH,
        )

    def copy3(j):
        return pltpu.make_async_remote_copy(
            src_ref=share.at[j, core, col, 1 - hi],
            dst_ref=land3.at[j],
            send_sem=s3.at[j],
            recv_sem=r3.at[j],
            device_id=(other_hi, me),
            device_id_type=MESH,
        )

    def straight(d):
        to = (coil + 2 * d) % coils
        return pltpu.make_async_remote_copy(
            src_ref=share.at[final, core, to // 4, to // 2 % 2],
            dst_ref=land4.at[d - 1],
            send_sem=s4.at[0],
            recv_sem=s4.at[1],
            device_id=(to, me),
            device_id_type=MESH,
        )

    def all4():
        return pltpu.make_async_remote_copy(
            src_ref=land4,
            dst_ref=land4,
            send_sem=s4.at[0],
            recv_sem=s4.at[1],
            device_id=(other_hi, me),
            device_id_type=MESH,
        )

    def step2(x):
        copy1(x).wait_recv()
        share[x, core] = share[x, core] + land1[x]

        def usual():
            for d in range(1, ring):
                copy2(x, d).start()

        def direct():
            for d in range(1, coils // 2):
                straight(d).start()

        if isinstance(x, int) and x == final:
            direct()
        else:
            usual()

    def sum3(x):
        all2(x).wait_recv()
        total = share[x, core, col]
        for d in range(ring - 1):
            total = total + land2[x, d]
        share[x, core, col] = total

    def send3(x):
        copy3(x).start()

    def finish(x):
        copy3(x).wait_recv()
        total = share[x, core, col, hi] + land3[x]
        for comp in range(2):
            out_ref[comp, x] = total[comp]

    def finish_last():
        all4().wait_recv()
        total = share[final, core, col, hi]
        for d in range(coils // 2 - 1):
            total = total + land4[d]
        for comp in range(2):
            out_ref[comp, final] = total[comp]

    last = chunks - 1
    final = chunks * WIDE - 1

    def early(j):
        readout(j)

        @pl.when(j < last)
        def _():
            send(j * WIDE, 2)

        @pl.when(j == last)
        def _():
            send(j * WIDE, 1)
            send(j * WIDE + 1, 1)

    readout(0)
    pl.semaphore_wait(barrier, pencils - 1 + coils // 2)
    send(0, 2)
    readout(1)
    send(2, 2)
    for load in loads[2:]:
        load.wait()

    def turn(j, carry):
        x = j * WIDE

        @pl.when(j + 2 <= last)
        def _():
            early(j + 2)

        @pl.when(j < last)
        def _():
            a_many(x, 2).wait_recv()

        @pl.when(j == last)
        def _():
            a_many(x, 1).wait_recv()

        compute(x, 0)

        @pl.when(j >= 1)
        def _():
            step2(x - 1)

        @pl.when(j == last)
        def _():
            for k in (3, 2):
                sum3(x - k)
                send3(x - k)
            a_many(x + 1, 1).wait_recv()

        compute(x + 1, 1)
        step2(x)

        @pl.when((j >= 2) & (j < last))
        def _():
            sum3(x - 3)
            send3(x - 3)

        @pl.when((j >= 1) & (j < last))
        def _():
            sum3(x - 2)
            send3(x - 2)

        return carry

    lax.fori_loop(0, chunks, turn, 0)
    x = last * WIDE
    for k in range(x - 3):
        finish(k)
    step2(final)
    for k in (x - 1, x):
        sum3(k)
        send3(k)
    for k in range(x - 3, x):
        finish(k)

    def drain(j, carry):
        copy1(j).wait_send()
        all2(j).wait_send()
        copy3(j).wait_send()
        return carry

    for j in range(last):
        a_many(j * WIDE, 2).wait_send()
    a_many(x, 1).wait_send()
    a_many(x + 1, 1).wait_send()
    lax.fori_loop(0, x, drain, 0)
    finish(x)
    finish_last()
    drain(x, 0)
    copy1(final).wait_send()
    all4().wait_send()


def on_device(coils, pencils, kspace, sensitivity, line_index):
    _, coil_dev, part_dev, lines, nx = kspace.shape
    slab, ny, nz = sensitivity.shape[2:]
    chunks = slab // WIDE
    ring = coils // 4
    deep = ny // coils
    sizes = (pencils, coils, chunks, nx, ny, nz, lines)
    scale = 1.0 / math.sqrt(nx * ny * nz)
    rows = part_dev * lines
    wx = jnp.asarray(readout_table(nx, pencils))
    wy = jnp.asarray(phase_table(ny, lines, coils))
    wz = jnp.asarray(partition_table(nz, scale))
    block = (2, deep, nz)
    vmem = pltpu.VMEM
    dma = pltpu.SemaphoreType.DMA
    flat = kspace.reshape(2, coil_dev, rows, nx)
    return pl.pallas_call(
        functools.partial(kernel, sizes),
        out_shape=jax.ShapeDtypeStruct((2, slab, deep, nz), F32),
        in_specs=[
            pl.BlockSpec(memory_space=pl.ANY),
            pl.BlockSpec(memory_space=pl.ANY),
            pl.BlockSpec(memory_space=pltpu.VMEM),
            pl.BlockSpec(memory_space=pl.ANY),
            pl.BlockSpec(memory_space=pl.ANY),
            pl.BlockSpec(memory_space=pl.ANY),
        ],
        out_specs=pl.BlockSpec(memory_space=pltpu.VMEM),
        scratch_shapes=[
            vmem(flat.shape, F32),
            vmem(sensitivity.shape, BF16),
            vmem(wx.shape, BF16),
            vmem(wy.shape, BF16),
            vmem(wz.shape, BF16),
            vmem((coil_dev, rows, 6 * nx), BF16),
            vmem((nz, 2 * lines), jnp.int32),
            vmem((slab, pencils * BLOCK, 128), F32),
            vmem((slab, pencils * BLOCK, 128), F32),
            vmem((WIDE, coil_dev * nz, 6 * ny), BF16),
            vmem((2 * ny, coil_dev * nz), F32),
            vmem((2 * ny, 6 * nz), BF16),
            vmem((slab, 2, ring, 2) + block, F32),
            vmem((slab, ring, 2) + block, F32),
            vmem((slab, ring - 1, 2) + block, F32),
            vmem((slab,) + block, F32),
            vmem((coils // 2 - 1,) + block, F32),
            dma((5,)),
        ]
        + [dma((slab,)) for _ in range(8)]
        + [dma((2,))],
        compiler_params=pltpu.CompilerParams(
            collective_id=0, has_side_effects=True, vmem_limit_bytes=62 * 1024 * 1024
        ),
    )(flat, sensitivity, line_index.T, wx, wy, wz)


def solution(mesh):
    in_specs = (P(None, "coil", "pencil", None, None), P(None, "coil", "pencil", None, None), P())
    out_specs = P(None, "pencil", "coil", None)
    return jax.shard_map(
        functools.partial(on_device, mesh.shape["coil"], mesh.shape["pencil"]),
        mesh=mesh,
        in_specs=in_specs,
        out_specs=out_specs,
        check_vma=False,
    )
```

time: 72.3 us -> 57.3 us (0.79)
  Pallas kernels: 65.4 us -> 55.5 us
  local copies, waits for them, and re-layouts: 6.54 us -> 1.57 us
    pallas_call x1, Pallas kernels: 65.4 us -> 55.5 us  [on_device(): pl.pallas_call(functools.partial(kernel, sizes), out_shape=jax.ShapeDtype...]
    unnamed x10 -> x1, local copies, waits for them, and re-layouts: 6.54 us -> 1.57 us
where the time goes in v1:
time: 57.3 us; the launch traced here: 57.1 us
  Pallas kernels  55.5 us (97%)
  local copies, waits for them, and re-layouts  1.57 us (3%)
    pallas_call x1, Pallas kernels, on_device(): pl.pallas_call(functools.partial(kernel, sizes), out_shape=jax.ShapeDtype...  55.5 us
    unnamed x1, local copies, waits for them, and re-layouts  1.57 us

profile of v1, /device:TPU:1, one launch (start us, length us, event | category | flops | bytes accessed | tf_op | source)
XLA Modules:
  0.0 57.1 jit_solution(15015109992969884883)
XLA Ops:
  0.0 55.5 %shard_map.64 = f32[2,8,16,128]{3,2,1,0:T(8,128)} custom-call(f32[2,2,256,256]{3,2,1,0:T(8,128)} %bitcast.2, bf16[2,2,8,256,128]{4,3,2,1,0:T(8,128)(2,1)} %sens_hbm.1, s32[64,128]{1,0:T(8,128)} %bitcast.3, bf16[4,128,1536]{2,1,0:T(8,128)(2,1)} %constant.6.clone.wx_hbm, bf16[2,256,1536]{2,1,0:T(8,128)(2,1)} %constant.7.clone.wy_hbm, ...), custom_call_target="tpu_custom_call" | custom-call | tf_op jit(solution)/shard_map/pallas_call | solution.py:472
  55.5 1.6 %copy.8 = f32[2,8,16,128]{3,2,1,0:T(8,128)} copy(f32[2,8,16,128]{3,2,1,0:T(8,128)} %shard_map.64) | data formatting | bytes 262144

commit v2 on v1

--- a/solution.py
+++ b/solution.py
@@ -62,13 +62,14 @@
     sizes,
     kspace_hbm,
     sens_hbm,
-    lines_ref,
+    lines_hbm,
     wx_hbm,
     wy_hbm,
     wz_hbm,
     out_ref,
     kspace,
     sens,
+    lines_ref,
     wx,
     wy,
     wz,
@@ -106,11 +107,17 @@
     other_core = coil + 1 - 2 * core
     other_hi = coil + 2 - 4 * hi
 
+    pairs = [
+        (kspace_hbm, kspace),
+        (wx_hbm.at[0], wx.at[0]),
+        (wx_hbm.at[pl.ds(1, chunks - 1)], wx.at[pl.ds(1, chunks - 1)]),
+        (lines_hbm, lines_ref),
+        (wy_hbm, wy),
+        (wz_hbm, wz),
+        (sens_hbm, sens),
+    ]
     loads = [
-        pltpu.make_async_copy(src, dst, load_sem.at[i])
-        for i, (src, dst) in enumerate(
-            [(kspace_hbm, kspace), (wx_hbm, wx), (wy_hbm, wy), (wz_hbm, wz), (sens_hbm, sens)]
-        )
+        pltpu.make_async_copy(src, dst, load_sem.at[i]) for i, (src, dst) in enumerate(pairs)
     ]
     for load in loads[:2]:
         load.start()
@@ -130,9 +137,6 @@
     greet(other_core, me)
     for d in range(1, coils // 2):
         greet((coil + 2 * d) % coils, me)
-
-    here = lines_ref[...] - (ny // lines) * lax.broadcasted_iota(jnp.int32, (lines, nz), 0)
-    place[...] = jnp.concatenate([here, here], 0).T
 
     loads[0].wait()
     for load in loads[2:]:
@@ -220,41 +224,56 @@
                         grid[buf, rows, pl.ds(2 * ny + left, 128)] = high
                         grid[buf, rows, pl.ds(4 * ny + left, 128)] = low
 
-    def combine(x, buf):
+    def transform(buf, part, count):
         tall = ny // 2
-        table = wy[...].reshape(2 * ny, 6 * ny)
-        planes[...] = lax.dot_general(table, grid[buf], NT, preferred_element_type=F32)
-        for part in range(2):
+        top = part if count == 1 else 0
+        table = wy[pl.ds(top, count)].reshape(count * ny, 6 * ny)
+        planes[pl.ds(0, count * ny), :] = lax.dot_general(
+            table, grid[buf], NT, preferred_element_type=F32
+        )
+        for p in range(count):
             for c in range(2):
                 for comp in range(2):
-                    value = planes[pl.ds(part * ny + comp * tall, tall), pl.ds(c * nz, nz)]
+                    value = planes[pl.ds(p * ny + comp * tall, tall), pl.ds(c * nz, nz)]
                     high = value.astype(BF16)
                     low = (value - high.astype(F32)).astype(BF16)
-                    rows = pl.ds(part * ny + c * tall, tall)
+                    rows = pl.ds(p * ny + c * tall, tall)
                     mixed[rows, pl.ds(comp * nz, nz)] = high
                     mixed[rows, pl.ds((2 + comp) * nz, nz)] = high
                     mixed[rows, pl.ds((4 + comp) * nz, nz)] = low
-        image = jnp.dot(mixed[...], wz[...], preferred_element_type=F32)
-        for part in range(2):
+        return jnp.dot(mixed[pl.ds(0, count * ny), :], wz[...], preferred_element_type=F32)
+
+    def combine(x, buf, part, count):
+        image = transform(buf, part, count)
+        for p in range(count):
+            home = part if count == 1 else p
             for m in range(coils // 2):
                 real_part = 0.0
                 imag_part = 0.0
                 for c in range(2):
-                    top = part * ny + c * tall + m * deep
+                    top = p * ny + c * (ny // 2) + m * deep
                     re = image[top : top + deep, :nz]
                     im = image[top : top + deep, nz:]
-                    rows = pl.ds((2 * m + part) * deep, deep)
-                    sre = sens[0, c, x, rows, :].astype(F32)
-                    sim = sens[1, c, x, rows, :].astype(F32)
+                    first = (2 * m + home) * deep
+                    if count == 1:
+                        first = pl.multiple_of(first, deep)
+                    sre = sens[0, c, x, pl.ds(first, deep), :].astype(F32)
+                    sim = sens[1, c, x, pl.ds(first, deep), :].astype(F32)
                     real_part = real_part + sre * re + sim * im
                     imag_part = imag_part + sre * im - sim * re
-                share[x, part, m // 2, m % 2, 0] = real_part
-                share[x, part, m // 2, m % 2, 1] = imag_part
+                share[x, home, m // 2, m % 2, 0] = real_part
+                share[x, home, m // 2, m % 2, 1] = imag_part
 
     def compute(x, buf):
         fill(x, buf)
-        combine(x, buf)
+        combine(x, buf, 0, 2)
         copy1(x).start()
+
+    def compute_halves(x, buf):
+        fill(x, buf)
+        combine(x, buf, 1 - core, 1)
+        copy1(x).start()
+        combine(x, buf, core, 1)
 
     def copy1(j):
         return pltpu.make_async_remote_copy(
@@ -376,9 +395,14 @@
     readout(0)
     pl.semaphore_wait(barrier, pencils - 1 + coils // 2)
     send(0, 2)
+    loads[2].wait()
     readout(1)
     send(2, 2)
-    for load in loads[2:]:
+    loads[3].wait()
+    here = lines_ref[...] - (ny // lines) * lax.broadcasted_iota(jnp.int32, (lines, nz), 0)
+    place[...] = jnp.concatenate([here, here], 0).T
+
+    for load in loads[4:]:
         load.wait()
 
     def turn(j, carry):
@@ -388,50 +412,50 @@
         def _():
             early(j + 2)
 
-        @pl.when(j < last)
-        def _():
-            a_many(x, 2).wait_recv()
-
-        @pl.when(j == last)
-        def _():
-            a_many(x, 1).wait_recv()
-
-        compute(x, 0)
+        a_many(x, 2).wait_recv()
+        fill(x, 0)
+        fill(x + 1, 1)
+        combine(x, 0, 0, 2)
+        copy1(x).start()
 
         @pl.when(j >= 1)
         def _():
             step2(x - 1)
 
-        @pl.when(j == last)
-        def _():
-            for k in (3, 2):
-                sum3(x - k)
-                send3(x - k)
-            a_many(x + 1, 1).wait_recv()
-
-        compute(x + 1, 1)
+        combine(x + 1, 1, 0, 2)
+        copy1(x + 1).start()
         step2(x)
 
-        @pl.when((j >= 2) & (j < last))
+        @pl.when(j >= 2)
         def _():
             sum3(x - 3)
             send3(x - 3)
 
-        @pl.when((j >= 1) & (j < last))
+        @pl.when(j >= 1)
         def _():
             sum3(x - 2)
             send3(x - 2)
 
         return carry
 
-    lax.fori_loop(0, chunks, turn, 0)
+    lax.fori_loop(0, last, turn, 0)
     x = last * WIDE
+    a_many(x, 1).wait_recv()
+    compute(x, 0)
+    step2(x - 1)
+    for k in (3, 2):
+        sum3(x - k)
+        send3(x - k)
+    a_many(x + 1, 1).wait_recv()
+    step2(x)
+    compute_halves(final, 1)
+    sum3(x - 1)
+    send3(x - 1)
+    step2(final)
     for k in range(x - 3):
         finish(k)
-    step2(final)
-    for k in (x - 1, x):
-        sum3(k)
-        send3(k)
+    sum3(x)
+    send3(x)
     for k in range(x - 3, x):
         finish(k)
 
@@ -475,7 +499,7 @@
         in_specs=[
             pl.BlockSpec(memory_space=pl.ANY),
             pl.BlockSpec(memory_space=pl.ANY),
-            pl.BlockSpec(memory_space=pltpu.VMEM),
+            pl.BlockSpec(memory_space=pl.ANY),
             pl.BlockSpec(memory_space=pl.ANY),
             pl.BlockSpec(memory_space=pl.ANY),
             pl.BlockSpec(memory_space=pl.ANY),
@@ -484,6 +508,7 @@
         scratch_shapes=[
             vmem(flat.shape, F32),
             vmem(sensitivity.shape, BF16),
+            vmem(line_index.shape[::-1], jnp.int32),
             vmem(wx.shape, BF16),
             vmem(wy.shape, BF16),
             vmem(wz.shape, BF16),
@@ -499,7 +524,7 @@
             vmem((slab, ring - 1, 2) + block, F32),
             vmem((slab,) + block, F32),
             vmem((coils // 2 - 1,) + block, F32),
-            dma((5,)),
+            dma((7,)),
         ]
         + [dma((slab,)) for _ in range(8)]
         + [dma((2,))],

time: 57.3 us -> 55.9 us (0.976)
  Pallas kernels: 55.5 us -> 54.1 us
    pallas_call x1, Pallas kernels: 55.5 us -> 54.1 us  [on_device(): pl.pallas_call(functools.partial(kernel, sizes), out_shape=jax.ShapeDtype...]
where the time goes in v2:
time: 55.9 us; the launch traced here: 55.7 us
  Pallas kernels  54.1 us (97%)
  local copies, waits for them, and re-layouts  1.57 us (3%)
    pallas_call x1, Pallas kernels, on_device(): pl.pallas_call(functools.partial(kernel, sizes), out_shape=jax.ShapeDtype...  54.1 us
    unnamed x1, local copies, waits for them, and re-layouts  1.57 us

profile of v2, /device:TPU:1, one launch (start us, length us, event | category | flops | bytes accessed | tf_op | source)
XLA Modules:
  0.0 55.7 jit_solution(11547996178860173186)
XLA Ops:
  0.0 54.1 %shard_map.64 = f32[2,8,16,128]{3,2,1,0:T(8,128)} custom-call(f32[2,2,256,256]{3,2,1,0:T(8,128)} %bitcast.2, bf16[2,2,8,256,128]{4,3,2,1,0:T(8,128)(2,1)} %sens_hbm.1, s32[64,128]{1,0:T(8,128)} %bitcast.3, bf16[4,128,1536]{2,1,0:T(8,128)(2,1)} %constant.6.clone.wx_hbm, bf16[2,256,1536]{2,1,0:T(8,128)(2,1)} %constant.7.clone.wy_hbm, ...), custom_call_target="tpu_custom_call" | custom-call | tf_op jit(solution)/shard_map/pallas_call | solution.py:496
  54.2 1.6 %copy.8 = f32[2,8,16,128]{3,2,1,0:T(8,128)} copy(f32[2,8,16,128]{3,2,1,0:T(8,128)} %shard_map.64) | data formatting | bytes 262144

commit v3 on v2

--- a/solution.py
+++ b/solution.py
@@ -495,7 +495,7 @@
     flat = kspace.reshape(2, coil_dev, rows, nx)
     return pl.pallas_call(
         functools.partial(kernel, sizes),
-        out_shape=jax.ShapeDtypeStruct((2, slab, deep, nz), F32),
+        out_shape=vmem((2, slab, deep, nz), F32),
         in_specs=[
             pl.BlockSpec(memory_space=pl.ANY),
             pl.BlockSpec(memory_space=pl.ANY),

time: 55.9 us -> 54.3 us (0.971)
  local copies, waits for them, and re-layouts: 1.57 us -> 0.66 us
  Pallas kernels: 54.1 us -> 53.5 us
    unnamed x1, local copies, waits for them, and re-layouts: 1.57 us -> 0.66 us
    pallas_call x1, Pallas kernels: 54.1 us -> 53.5 us  [on_device(): pl.pallas_call(functools.partial(kernel, sizes), out_shape=vmem((2, slab,...]
where the time goes in v3:
time: 54.3 us; the launch traced here: 54.2 us
  Pallas kernels  53.5 us (99%)
  local copies, waits for them, and re-layouts  0.66 us (1%)
    pallas_call x1, Pallas kernels, on_device(): pl.pallas_call(functools.partial(kernel, sizes), out_shape=vmem((2, slab,...  53.5 us

profile of v3, /device:TPU:1, one launch (start us, length us, event | category | flops | bytes accessed | tf_op | source)
XLA Modules:
  0.0 54.2 jit_solution(8968605478284615999)
XLA Ops:
  0.0 53.5 %shard_map.64 = f32[2,8,16,128]{3,2,1,0:T(8,128)S(1)} custom-call(f32[2,2,256,256]{3,2,1,0:T(8,128)} %bitcast.2, bf16[2,2,8,256,128]{4,3,2,1,0:T(8,128)(2,1)} %sens_hbm.1, s32[64,128]{1,0:T(8,128)} %bitcast.3, bf16[4,128,1536]{2,1,0:T(8,128)(2,1)} %constant.6.clone.wx_hbm, bf16[2,256,1536]{2,1,0:T(8,128)(2,1)} %constant.7.clone.wy_hbm, ...), custom_call_target="tpu_custom_call" | custom-call | tf_op jit(solution)/shard_map/pallas_call | solution.py:496
  53.5 0.7 %copy.8 = f32[2,8,16,128]{3,2,1,0:T(8,128)} copy(f32[2,8,16,128]{3,2,1,0:T(8,128)S(1)} %shard_map.64) | data formatting | bytes 262144
